TPU v7x, 32 devices: a whole 2x2x4 slice. The times are simulated.
32 devices in a mesh: row: 4 (over y, x), col: 8 (over z, core).
Axes of the slice: x: 2, y: 2, z: 4, core: 2. Of those that a mesh axis runs over, the one named last changes fastest.
Arguments:
- fields: float32 [5, 1, 128, 2048], P(None, None, 'col', 'row'), may hold values from -3 to 150, as said below
Outputs:
- updated: float32 [5, 1, 128, 2048], P(None, None, 'col', 'row')
Inputs may be any that keep to these rules, and one draw needn't show every extreme that they name: `fields`: field 0 is the density and field 4 the total energy; density and pressure are positive in every cell.
All inputs are finite; a program needn't handle non-finite values.
Results may differ from a plain program's by a relative error of at most 0.0003.
Values sent between devices are 32-bit elements; how exact they have to be, the bound alone decides.
A program may use at most 64 MiB of HBM per device.

v0:
```python
import jax
import jax.numpy as jnp
from jax import lax
from jax.sharding import PartitionSpec as P

GAMMA = 1.4
COURANT = 0.3


def extended(shard, sides, width):
    for axis, dim in sides:
        count, length = (lax.axis_size(axis), shard.shape[dim])
        up = [(i, (i + 1) % count) for i in range(count)]
        down = [(j, i) for i, j in up]
        last = lax.slice_in_dim(shard, length - width, length, axis=dim)
        leading = lax.slice_in_dim(shard, 0, width, axis=dim)
        before = lax.ppermute(last, axis, up)
        after = lax.ppermute(leading, axis, down)
        shard = jnp.concatenate([before, shard, after], axis=dim)
    return shard


def window_slice(profile, begin_at, trim_end, direction_axis):
    direction_axis = direction_axis % profile.ndim
    return lax.slice_in_dim(
        profile, begin_at, profile.shape[direction_axis] - trim_end, axis=direction_axis
    )


def minmod(first_slope, second_slope):
    return (
        0.5
        * (jnp.sign(first_slope) + jnp.sign(second_slope))
        * jnp.minimum(jnp.abs(first_slope), jnp.abs(second_slope))
    )


def rebuild(profile, direction_axis):
    far_left = window_slice(profile, 0, 3, direction_axis)
    near_left = window_slice(profile, 1, 2, direction_axis)
    near_right = window_slice(profile, 2, 1, direction_axis)
    far_right = window_slice(profile, 3, 0, direction_axis)
    edge_value = 7.0 / 12.0 * (near_left + near_right) - 1.0 / 12.0 * (far_left + far_right)
    edge_value = jnp.clip(
        edge_value, jnp.minimum(near_left, near_right), jnp.maximum(near_left, near_right)
    )
    centre = window_slice(profile, 2, 2, direction_axis)
    lower_edge = window_slice(edge_value, 0, 1, direction_axis)
    upper_edge = window_slice(edge_value, 1, 0, direction_axis)
    upper_jump = upper_edge - centre
    lower_jump = centre - lower_edge
    right_face = centre + minmod(upper_jump, 2.0 * lower_jump)
    left_face = centre - minmod(lower_jump, 2.0 * upper_jump)
    return (
        window_slice(right_face, 0, 1, direction_axis),
        window_slice(left_face, 1, 0, direction_axis),
    )


def face_terms(density, velocity, pressure, normal):
    speed_square = velocity[0] * velocity[0] + velocity[1] * velocity[1] + velocity[2] * velocity[2]
    energy = pressure / (GAMMA - 1.0) + 0.5 * density * speed_square
    normal_speed = velocity[normal - 1]
    conserved = [
        density,
        density * velocity[0],
        density * velocity[1],
        density * velocity[2],
        energy,
    ]
    face_flux = [density * normal_speed]
    for component in range(3):
        momentum_flux = density * normal_speed * velocity[component]
        if component == normal - 1:
            momentum_flux = momentum_flux + pressure
        face_flux.append(momentum_flux)
    face_flux.append(normal_speed * (energy + pressure))
    signal = jnp.abs(normal_speed) + jnp.sqrt(GAMMA * pressure / density)
    return (conserved, face_flux, signal)


def primitives(cells):
    density = cells[0]
    velocity = [cells[1] / density, cells[2] / density, cells[3] / density]
    kinetic = (
        0.5
        * density
        * (velocity[0] * velocity[0] + velocity[1] * velocity[1] + velocity[2] * velocity[2])
    )
    pressure = (GAMMA - 1.0) * (cells[4] - kinetic)
    return (density, velocity, pressure)


def courant(cells):
    density, velocity, pressure = primitives(cells)
    return jnp.maximum(jnp.abs(velocity[0]), jnp.abs(velocity[1])) + jnp.sqrt(
        GAMMA * pressure / density
    )


def sweep_along(padded, time_step, direction_axis, normal):
    density, velocity, pressure = primitives(padded)
    face_pairs = [
        rebuild(profile, direction_axis)
        for profile in [density, velocity[0], velocity[1], velocity[2], pressure]
    ]
    left_states = [pair[0] for pair in face_pairs]
    right_states = [pair[1] for pair in face_pairs]
    left_conserved, left_flux, left_signal = face_terms(
        left_states[0], left_states[1:4], left_states[4], normal
    )
    right_conserved, right_flux, right_signal = face_terms(
        right_states[0], right_states[1:4], right_states[4], normal
    )
    signal = jnp.maximum(left_signal, right_signal)
    results = []
    for component in range(5):
        face_flux = 0.5 * (left_flux[component] + right_flux[component]) - 0.5 * signal * (
            right_conserved[component] - left_conserved[component]
        )
        difference = window_slice(face_flux, 1, 0, direction_axis) - window_slice(
            face_flux, 0, 1, direction_axis
        )
        results.append(
            window_slice(padded[component], 3, 3, direction_axis) - time_step * difference
        )
    return jnp.stack(results)


def local(fields):
    local_peak = jnp.max(courant(fields))
    peak_speed = lax.pmax(local_peak, ("row", "col"))
    time_step = COURANT / peak_speed
    padded = extended(fields, (("row", 3),), 3)
    block_fields = sweep_along(padded, time_step, -1, 1)
    padded = extended(block_fields, (("col", 2),), 3)
    return sweep_along(padded, time_step, -2, 2)


def solution(mesh):
    in_specs = (P(None, None, "col", "row"),)
    out_specs = P(None, None, "col", "row")
    return jax.shard_map(local, mesh=mesh, in_specs=in_specs, out_specs=out_specs, check_vma=False)
```

profile of v0, /device:TPU:0, one launch (start us, length us, event | category | flops | bytes accessed | tf_op | source)
XLA Modules:
  0.0 56.6 jit_solution(11483369013103228687)
XLA Ops:
  0.0 0.9 %fusion.99 = (f32[5,1,16,3]{3,2,1,0:T(8,128)S(1)}, f32[5,1,16,3]{3,2,1,0:T(8,128)S(1)}) fusion(f32[5,1,16,512]{3,2,1,0:T(8,128)} %param.1), kind=kLoop, calls=%fused_computation.204 | loop fusion | bytes 3840 | tf_op jit(solution)/shard_map/slice | solution.py:15
  0.9 2.9 %collective-permute-start = (f32[5,1,16,3]{3,2,1,0:T(8,128)S(1)}, f32[5,1,16,3]{3,2,1,0:T(8,128)S(1)}, u32[]{:S(2)}, u32[]{:S(2)}) collective-permute-start(f32[5,1,16,3]{3,2,1,0:T(8,128)S(1)} %get-tuple-element.47), channel_id=1, source_target_pairs={{0,8},{8,16},{16,24},{24,0},{1,9},{9,17},{17,25},{25,1},{2,10},{10... | collective-permute-start | bytes 2888 | tf_op jit(solution)/shard_map/ppermute | solution.py:17
  3.9 1.0 %collective-permute-start.1 = (f32[5,1,16,3]{3,2,1,0:T(8,128)S(1)}, f32[5,1,16,3]{3,2,1,0:T(8,128)S(1)}, u32[]{:S(2)}, u32[]{:S(2)}) collective-permute-start(f32[5,1,16,3]{3,2,1,0:T(8,128)S(1)} %get-tuple-element.48), channel_id=1, source_target_pairs={{8,0},{16,8},{24,16},{0,24},{9,1},{17,9},{25,17},{1,25},{10,2},{18... | collective-permute-start | bytes 2888 | tf_op jit(solution)/shard_map/ppermute | solution.py:18
  4.9 0.6 %add_reduce_fusion = f32[]{:T(128)} fusion(f32[5,1,16,512]{3,2,1,0:T(8,128)S(1)} %copy-done), kind=kLoop, calls=%fused_computation.196 | loop fusion | flops 147455 | bytes 163844 | tf_op jit(solution)/shard_map/reduce_max | solution.py:131
  5.5 40.3 %pmax.7 = f32[]{:T(128)} all-reduce(f32[]{:T(128)} %add_reduce_fusion), channel_id=1, replica_groups=mesh['row'=4,'col'=8] {'row','col'}, use_global_device_ids=true, to_apply=%region_1.0 | all-reduce | flops 1 | bytes 8 | tf_op jit(solution)/shard_map/pmax | solution.py:132
  46.5 0.0 collective-permute-done
  46.5 0.0 collective-permute-done.1
  46.5 0.1 pad_maximum_fusion.1
  46.7 0.1 fusion.39
  46.8 0.1 fusion.31
  46.9 0.1 fusion.27
  47.0 0.1 fusion.23
  47.1 0.1 fusion.35
  47.2 0.1 slice_subtract_fusion.29
  47.3 0.1 slice_subtract_fusion.23
  47.4 0.1 slice_subtract_fusion.17
  47.6 0.4 multiply_subtract_fusion.5
  48.0 0.2 multiply_subtract_fusion.6
  48.2 0.1 fusion.79
  48.3 0.1 fusion.75
  48.4 0.1 fusion.71
  48.5 0.1 fusion.67
  48.6 0.1 fusion.63
  48.7 0.1 collective-permute-start.2
  48.8 3.5 %collective-permute-start.3 = (f32[5,1,3,512]{3,2,1,0:T(4,128)S(1)}, f32[5,1,3,512]{3,2,1,0:T(4,128)S(1)}, u32[]{:S(2)}, u32[]{:S(2)}) collective-permute-start(f32[5,1,3,512]{3,2,1,0:T(4,128)S(1)} %get-tuple-element.46), channel_id=1, source_target_pairs={{1,0},{2,1},{3,2},{4,3},{5,4},{6,5},{7,6},{0,7},{9,8},{10,9},{11,1... | collective-permute-start | bytes 92168 | tf_op jit(solution)/shard_map/ppermute | solution.py:18
  52.3 1.7 %collective-permute-done.2 = f32[5,1,3,512]{3,2,1,0:T(4,128)S(1)} collective-permute-done((f32[5,1,3,512]{3,2,1,0:T(4,128)S(1)}, f32[5,1,3,512]{3,2,1,0:T(4,128)S(1)}, u32[]{:S(2)}, u32[]{:S(2)}) %collective-permute-start.2) | collective-permute-done | bytes 30752 | tf_op jit(solution)/shard_map/ppermute | solution.py:17
  54.0 0.0 collective-permute-done.3
  54.4 0.5 multiply_subtract_fusion
  55.0 0.3 multiply_subtract_fusion.1
  55.3 0.0 copy-start.1
  55.3 0.7 %copy-done.1 = f32[5,1,16,512]{3,2,1,0:T(8,128)} copy-done((f32[5,1,16,512]{3,2,1,0:T(8,128)}, f32[5,1,16,512]{3,2,1,0:T(8,128)S(1)}, u32[]{:S(2)}) %copy-start.1) | copy-done | bytes 163864
  56.0 0.6 %fusion.43 = f32[5,1,16,512]{3,2,1,0:T(8,128)} fusion(f32[5,1,16,512]{3,2,1,0:T(8,128)} %copy-done.1, f32[1,17,512]{2,1,0:T(8,128)S(1)} %get-tuple-element.5, f32[1,22,512]{2,1,0:T(8,128)S(1)} %get-tuple-element.31, f32[]{:T(128)S(6)} %div.165), kind=kLoop, calls=%fused_computation.140 | loop fusion | flops 24576 | bytes 131076 | tf_op jit(solution)/shard_map/stack | solution.py:127
  (22 shorter events, 0.5 us)
Async XLA Ops:
  0.0 4.9 %copy-start = (f32[5,1,16,512]{3,2,1,0:T(8,128)S(1)}, f32[5,1,16,512]{3,2,1,0:T(8,128)}, u32[]{:S(2)}) copy-start(f32[5,1,16,512]{3,2,1,0:T(8,128)} %param.1) | copy-start | bytes 491524
  0.9 45.5 %collective-permute-start = (f32[5,1,16,3]{3,2,1,0:T(8,128)S(1)}, f32[5,1,16,3]{3,2,1,0:T(8,128)S(1)}, u32[]{:S(2)}, u32[]{:S(2)}) collective-permute-start(f32[5,1,16,3]{3,2,1,0:T(8,128)S(1)} %get-tuple-element.47), channel_id=1, source_target_pairs={{0,8},{8,16},{16,24},{24,0},{1,9},{9,17},{17,25},{25,1},{2,10},{10... | collective-permute-start | bytes 2888 | tf_op jit(solution)/shard_map/ppermute | solution.py:17
  3.9 42.6 %collective-permute-start.1 = (f32[5,1,16,3]{3,2,1,0:T(8,128)S(1)}, f32[5,1,16,3]{3,2,1,0:T(8,128)S(1)}, u32[]{:S(2)}, u32[]{:S(2)}) collective-permute-start(f32[5,1,16,3]{3,2,1,0:T(8,128)S(1)} %get-tuple-element.48), channel_id=1, source_target_pairs={{8,0},{16,8},{24,16},{0,24},{9,1},{17,9},{25,17},{1,25},{10,2},{18... | collective-permute-start | bytes 2888 | tf_op jit(solution)/shard_map/ppermute | solution.py:18
  48.7 5.3 %collective-permute-start.2 = (f32[5,1,3,512]{3,2,1,0:T(4,128)S(1)}, f32[5,1,3,512]{3,2,1,0:T(4,128)S(1)}, u32[]{:S(2)}, u32[]{:S(2)}) collective-permute-start(f32[5,1,3,512]{3,2,1,0:T(4,128)S(1)} %get-tuple-element.45), channel_id=1, source_target_pairs={{0,1},{1,2},{2,3},{3,4},{4,5},{5,6},{6,7},{7,0},{8,9},{9,10},{10,1... | collective-permute-start | bytes 92168 | tf_op jit(solution)/shard_map/ppermute | solution.py:17
  48.8 5.3 %collective-permute-start.3 = (f32[5,1,3,512]{3,2,1,0:T(4,128)S(1)}, f32[5,1,3,512]{3,2,1,0:T(4,128)S(1)}, u32[]{:S(2)}, u32[]{:S(2)}) collective-permute-start(f32[5,1,3,512]{3,2,1,0:T(4,128)S(1)} %get-tuple-element.46), channel_id=1, source_target_pairs={{1,0},{2,1},{3,2},{4,3},{5,4},{6,5},{7,6},{0,7},{9,8},{10,9},{11,1... | collective-permute-start | bytes 92168 | tf_op jit(solution)/shard_map/ppermute | solution.py:18
  55.3 0.7 %copy-start.1 = (f32[5,1,16,512]{3,2,1,0:T(8,128)}, f32[5,1,16,512]{3,2,1,0:T(8,128)S(1)}, u32[]{:S(2)}) copy-start(f32[5,1,16,512]{3,2,1,0:T(8,128)S(1)} %fusion.47) | copy-start | bytes 491524
where the time goes:
time: 57 us; the launch traced here: 56.6 us
  blocking collectives  40.3 us (71%)
  starting transfers between devices  7.54 us (13%)
  other arithmetic  4.44 us (8%)
  waiting for transfers between devices  1.73 us (3%)
  local copies, waits for them, and re-layouts  1.64 us (3%)
  between operations  0.99 us (2%)
    pmax x1, blocking collectives, local(): peak_speed = lax.pmax(local_peak, ('row', 'col'))  40.3 us
    ppermute x2, starting transfers between devices, extended(): after = lax.ppermute(leading, axis, down)  4.54 us
    ppermute x2, starting transfers between devices, extended(): before = lax.ppermute(last, axis, up)  3 us
    ppermute x2, waiting for transfers between devices, extended(): before = lax.ppermute(last, axis, up)  1.73 us
    sub x4, other arithmetic, sweep_along(): 0.5 * (left_flux[component] + right_flux[component])  1.42 us
  transfers between devices with their start and end apart: 4, of which 1 were waited for; matrix products, arithmetic and copies ran while one was open for 1% of the time, Pallas kernels for 0%

commit v1 on v0

v1 whole, which is shorter than its diff:
```python
import functools

import jax
import jax.numpy as jnp
from jax import lax
from jax.experimental import pallas as pl
from jax.experimental.pallas import tpu as pltpu
from jax.sharding import PartitionSpec as P

GAMMA = 1.4
COURANT = 0.3
MESH = pl.DeviceIdType.MESH
LANES = 128
SUBLANES = 8
TINY = 1e-37


def inverse(value):
    guess = pl.reciprocal(value, approx=True)
    return guess * (2.0 - value * guess)


def root(value):
    return value * lax.rsqrt(jnp.maximum(value, TINY))


def primitives(cells):
    density = cells[0]
    inverse_density = inverse(density)
    velocity = [cells[k] * inverse_density for k in (1, 2, 3)]
    square = velocity[0] * velocity[0] + velocity[1] * velocity[1] + velocity[2] * velocity[2]
    pressure = (GAMMA - 1.0) * (cells[4] - 0.5 * density * square)
    return [density] + velocity + [pressure], inverse_density


def limited(first, second):
    return jnp.minimum(jnp.maximum(first, jnp.minimum(second, 0.0)), jnp.maximum(second, 0.0))


def face_values(q, up, down):
    after = up(q)
    edge = 7.0 / 12.0 * (q + after) - 1.0 / 12.0 * (down(q) + up(after))
    edge = jnp.minimum(jnp.maximum(edge, jnp.minimum(q, after)), jnp.maximum(q, after))
    rise = edge - q
    fall = q - down(edge)
    right = q + limited(rise, fall + fall)
    left = q - limited(fall, rise + rise)
    return right, up(left)


def face_terms(state, normal):
    density, pressure = state[0], state[4]
    velocity = state[1:4]
    square = velocity[0] * velocity[0] + velocity[1] * velocity[1] + velocity[2] * velocity[2]
    energy = pressure * (1.0 / (GAMMA - 1.0)) + 0.5 * density * square
    speed = velocity[normal - 1]
    momentum = [density * v for v in velocity]
    mass_flux = momentum[normal - 1]
    flux = [mass_flux] + [mass_flux * v for v in velocity] + [speed * (energy + pressure)]
    flux[normal] = flux[normal] + pressure
    signal = jnp.abs(speed) + root(GAMMA * pressure * inverse(density))
    return [density] + momentum + [energy], flux, signal


def flux_differences(profiles, up, down, normal):
    pairs = [face_values(q, up, down) for q in profiles]
    left_cons, left_flux, left_signal = face_terms([a for a, _ in pairs], normal)
    right_cons, right_flux, right_signal = face_terms([b for _, b in pairs], normal)
    signal = jnp.maximum(left_signal, right_signal)
    results = []
    for k in range(5):
        flux = (left_flux[k] + right_flux[k]) - signal * (right_cons[k] - left_cons[k])
        results.append(flux - down(flux))
    return results


def shifts(length, axis):
    return (
        lambda a: pltpu.roll(a, length - 1, axis),
        lambda a: pltpu.roll(a, 1, axis),
    )


def kernel(
    rows, cols, x, out, u, df, prim, xr, xl, yt, yb, rxl, rxr, rya, ryb, rc, m0, m1, m1s, m2,
    in_sem, halo_send, halo_recv, row_send, row_recv, col_send, col_recv,
):
    ny, nx = x.shape[2], x.shape[3]
    me_r, me_c = lax.axis_index("row"), lax.axis_index("col")

    def row_at(step):
        return lax.rem(me_r + (step % rows), rows)

    def col_at(step):
        return lax.rem(me_c + (step % cols), cols)

    load = pltpu.make_async_copy(x.at[:, 0], u.at[:, pl.ds(0, ny)], in_sem)
    load.start()

    barrier = pltpu.get_barrier_semaphore()
    peers = [(row_at(d), me_c) for d in range(1, rows)]
    peers += [(me_r, col_at(d)) for d in range(1, cols)]
    peers += [(row_at(a), col_at(b)) for a in (1, -1) for b in (1, -1)]
    for peer in peers:
        pl.semaphore_signal(barrier, inc=1, device_id=peer, device_id_type=MESH)
    load.wait()

    peak = None
    for r in range(0, ny, SUBLANES):
        profiles, inverse_density = primitives([u[f, r : r + SUBLANES, :] for f in range(5)])
        for f in range(5):
            prim[f, r : r + SUBLANES, :] = profiles[f]
        speed = jnp.maximum(jnp.abs(profiles[1]), jnp.abs(profiles[2]))
        speed = speed + root(GAMMA * profiles[4] * inverse_density)
        for c in range(0, nx, LANES):
            part = speed[:, c : c + LANES]
            peak = part if peak is None else jnp.maximum(peak, part)
    m0[...] = peak
    pl.semaphore_wait(barrier, len(peers))

    sends = []

    def send(src, dst, send_sem, recv_sem, device):
        copy = pltpu.make_async_remote_copy(
            src_ref=src, dst_ref=dst, send_sem=send_sem, recv_sem=recv_sem,
            device_id=device, device_id_type=MESH,
        )
        copy.start()
        sends.append(copy)
        return copy

    for d in range(1, rows):
        send(m0, m1.at[d - 1], row_send.at[d - 1], row_recv, (row_at(d), me_c))

    lane = lax.broadcasted_iota(jnp.int32, (ny, LANES), 1)
    pack_r = pack_l = None
    for f in range(5):
        edge_r = pltpu.roll(u[f, 0:ny, nx - LANES : nx], 8 * f + 3, 1)
        edge_l = u[f, 0:ny, 0:LANES]
        if f:
            edge_l = pltpu.roll(edge_l, 8 * f, 1)
            pack_r = jnp.where(lane < 8 * f, pack_r, edge_r)
            pack_l = jnp.where(lane < 8 * f, pack_l, edge_l)
        else:
            pack_r, pack_l = edge_r, edge_l
    xr[...] = pack_r
    xl[...] = pack_l
    for f in range(5):
        yt[3 * f : 3 * f + 3, :] = u[f, 0:3, :]
        yb[3 * f : 3 * f + 3, :] = u[f, ny - 3 : ny, :]
    yt[15:16, :] = u[0, 0:1, :]
    yb[15:16, :] = u[0, 0:1, :]
    top, bottom = pl.ds(0, SUBLANES), pl.ds(ny - SUBLANES, SUBLANES)
    halos = []
    for i, (src, dst, device) in enumerate(
        [
            (yb, rya, (me_r, col_at(1))),
            (yt, ryb, (me_r, col_at(-1))),
            (xr, rxl, (row_at(1), me_c)),
            (xl, rxr, (row_at(-1), me_c)),
            (xr.at[bottom], rc.at[0], (row_at(1), col_at(1))),
            (xl.at[bottom], rc.at[1], (row_at(-1), col_at(1))),
            (xr.at[top], rc.at[2], (row_at(1), col_at(-1))),
            (xl.at[top], rc.at[3], (row_at(-1), col_at(-1))),
        ]
    ):
        halos.append(send(src, dst, halo_send.at[i], halo_recv.at[i], device))

    pltpu.make_async_copy(m1, m1, row_recv).wait()
    peak = m0[...]
    for d in range(rows - 1):
        peak = jnp.maximum(peak, m1[d])
    m1s[...] = peak
    for d in range(1, cols):
        send(m1s, m2.at[d - 1], col_send.at[d - 1], col_recv, (me_r, col_at(d)))

    up, down = shifts(nx, 1)
    for r in range(0, ny, SUBLANES):
        profiles = [prim[f, r : r + SUBLANES, :] for f in range(5)]
        for f, difference in enumerate(flux_differences(profiles, up, down, 1)):
            df[f, r : r + SUBLANES, :] = difference

    halos[0].wait_recv()
    halos[1].wait_recv()
    for f in range(5):
        u[f, ny : ny + 3, :] = ryb[3 * f : 3 * f + 3, :]
        u[f, ny + 3 : ny + 5, :] = u[f, 3:5, :]
        u[f, ny + 5 : ny + 8, :] = rya[3 * f : 3 * f + 3, :]
    profiles, _ = primitives([u[f, ny : ny + SUBLANES, :] for f in range(5)])
    for f, difference in enumerate(flux_differences(profiles, up, down, 1)):
        df[f, ny : ny + SUBLANES, :] = difference

    for copy in halos[2:]:
        copy.wait_recv()
    total = ny + SUBLANES
    lane = lax.broadcasted_iota(jnp.int32, (total, LANES), 1)
    below = lax.broadcasted_iota(jnp.int32, (SUBLANES, LANES), 0) < 4
    far_left = jnp.concatenate([rxl[...], jnp.where(below, rc[2], rc[0])], axis=0)
    far_right = jnp.concatenate([rxr[...], jnp.where(below, rc[3], rc[1])], axis=0)
    seam = []
    for f in range(5):
        begin = u[f, :, 0:LANES]
        end = pltpu.roll(u[f, :, nx - LANES : nx], 64, 1)
        before = pltpu.roll(far_left, 125 - 8 * f, 1)
        after = pltpu.roll(far_right, 64 - 8 * f, 1)
        tile = jnp.where(lane < 32, begin, end)
        tile = jnp.where(lane >= 125, before, tile)
        seam.append(jnp.where((lane >= 64) & (lane < 67), after, tile))
    profiles, _ = primitives(seam)
    up, down = shifts(LANES, 1)
    for f, difference in enumerate(flux_differences(profiles, up, down, 1)):
        df[f, :, 0:LANES] = jnp.where(lane < 3, difference, df[f, :, 0:LANES])
        df[f, :, nx - LANES : nx] = jnp.where(
            lane >= 125, pltpu.roll(difference, 64, 1), df[f, :, nx - LANES : nx]
        )

    pltpu.make_async_copy(m2, m2, col_recv).wait()
    for d in range(cols - 1):
        peak = jnp.maximum(peak, m2[d])
    peak = jnp.max(jnp.max(peak, axis=0, keepdims=True), axis=1, keepdims=True)
    half_step = (0.5 * COURANT) / peak

    up, down = shifts(total, 0)
    for c in range(0, nx, LANES):
        cells = [
            u[f, :, c : c + LANES] - half_step * df[f, :, c : c + LANES] for f in range(5)
        ]
        profiles, _ = primitives(cells)
        for f, difference in enumerate(flux_differences(profiles, up, down, 2)):
            result = cells[f] - half_step * difference
            out[f, 0, :, c : c + LANES] = result[0:ny]

    for copy in sends:
        copy.wait_send()


def local(rows, cols, fields):
    ny, nx = fields.shape[2], fields.shape[3]
    vmem = lambda *shape: pltpu.VMEM(shape, jnp.float32)
    dma = pltpu.SemaphoreType.DMA
    return pl.pallas_call(
        functools.partial(kernel, rows, cols),
        out_shape=jax.ShapeDtypeStruct(fields.shape, fields.dtype),
        in_specs=[pl.BlockSpec(memory_space=pl.ANY)],
        out_specs=pl.BlockSpec(memory_space=pltpu.VMEM),
        scratch_shapes=[
            vmem(5, ny + SUBLANES, nx),
            vmem(5, ny + SUBLANES, nx),
            vmem(5, ny, nx),
            vmem(ny, LANES),
            vmem(ny, LANES),
            vmem(16, nx),
            vmem(16, nx),
            vmem(ny, LANES),
            vmem(ny, LANES),
            vmem(16, nx),
            vmem(16, nx),
            vmem(4, SUBLANES, LANES),
            vmem(SUBLANES, LANES),
            vmem(rows - 1, SUBLANES, LANES),
            vmem(SUBLANES, LANES),
            vmem(cols - 1, SUBLANES, LANES),
            dma,
            dma((8,)),
            dma((8,)),
            dma((rows - 1,)),
            dma,
            dma((cols - 1,)),
            dma,
        ],
        compiler_params=pltpu.CompilerParams(
            collective_id=0, has_side_effects=True, vmem_limit_bytes=32 * 1024 * 1024
        ),
        name="sweeps",
    )(fields)


def solution(mesh):
    spec = P(None, None, "col", "row")
    return jax.shard_map(
        functools.partial(local, mesh.shape["row"], mesh.shape["col"]),
        mesh=mesh,
        in_specs=(spec,),
        out_specs=spec,
        check_vma=False,
    )
```

time: 57 us -> 14.5 us (0.25)
  blocking collectives: 40.3 us -> 0 us
  Pallas kernels: 0 us -> 12.8 us
  starting transfers between devices: 7.54 us -> 0 us
  other arithmetic: 4.44 us -> 0 us
  waiting for transfers between devices: 1.73 us -> 0 us
  between operations: 0.99 us -> 0.01 us
    pmax x1 -> x0, blocking collectives: 40.3 us -> none  [local(): peak_speed = lax.pmax(local_peak, ('row', 'col'))]
    pallas_call x0 -> x1, Pallas kernels: none -> 12.8 us  [local(): pl.pallas_call(functools.partial(kernel, rows, cols), out_shape=jax.Shape...]
    ppermute x4 -> x0, starting transfers between devices: 7.54 us -> none  [the longest x2 4.54 us: extended(): after = lax.ppermute(leading, axis, down)]
    sub x12 -> x0, other arithmetic: 1.81 us -> none  [the longest x4 1.42 us: sweep_along(): 0.5 * (left_flux[component] + right_flux[component])]
    ppermute x4 -> x0, waiting for transfers between devices: 1.73 us -> none  [the longest x2 1.73 us: extended(): before = lax.ppermute(last, axis, up)]
    slice x2 -> x0, local copies, waits for them, and re-layouts: 0.94 us -> none  [extended(): last = lax.slice_in_dim(shard, length - width, length, axis=dim)]
    unnamed x4 -> x3, local copies, waits for them, and re-layouts: 0.66 us -> 1.58 us
    another operation x2 -> x0, other arithmetic: 0.71 us -> none  [sweep_along(): return jnp.stack(results)]
  transfers between devices with their start and end apart: 4 -> 0, of which waited for: 1 -> 0; matrix products, arithmetic and copies ran while one was open for 1% -> 0% of each run, Pallas kernels for 0% -> 0%
where the time goes in v1:
time: 14.5 us; the launch traced here: 14.4 us
  Pallas kernels  12.8 us (88%)
  local copies, waits for them, and re-layouts  1.58 us (11%)
    pallas_call x1, Pallas kernels, local(): pl.pallas_call(functools.partial(kernel, rows, cols), out_shape=jax.Shape...  12.8 us
    unnamed x3, local copies, waits for them, and re-layouts  1.58 us

profile of v1, /device:TPU:0, one launch (start us, length us, event | category | flops | bytes accessed | tf_op | source)
XLA Modules:
  0.0 14.4 jit_solution(17631911400460671250)
XLA Ops:
  0.0 0.0 copy-start
  0.0 0.9 %copy-done = f32[5,1,16,512]{3,2,1,0:T(8,128)S(1)} copy-done((f32[5,1,16,512]{3,2,1,0:T(8,128)S(1)}, f32[5,1,16,512]{3,2,1,0:T(8,128)}, u32[]{:S(2)}) %copy-start) | copy-done | bytes 163864
  0.9 12.8 %sweeps.1 = f32[5,1,16,512]{3,2,1,0:T(8,128)S(1)} custom-call(f32[5,1,16,512]{3,2,1,0:T(8,128)S(1)} %copy-done), custom_call_target="tpu_custom_call" | custom-call | tf_op jit(solution)/shard_map/sweeps/pallas_call | solution.py:241
  13.7 0.7 %copy.3 = f32[5,1,16,512]{3,2,1,0:T(8,128)} copy(f32[5,1,16,512]{3,2,1,0:T(8,128)S(1)} %sweeps.1) | data formatting | bytes 327680
Async XLA Ops:
  0.0 0.9 %copy-start = (f32[5,1,16,512]{3,2,1,0:T(8,128)S(1)}, f32[5,1,16,512]{3,2,1,0:T(8,128)}, u32[]{:S(2)}) copy-start(f32[5,1,16,512]{3,2,1,0:T(8,128)} %x.1) | copy-start | bytes 491524

commit v2 on v1

--- a/solution.py
+++ b/solution.py
@@ -82,8 +82,8 @@
 
 
 def kernel(
-    rows, cols, x, out, u, df, prim, xr, xl, yt, yb, rxl, rxr, rya, ryb, rc, m0, m1, m1s, m2,
-    in_sem, halo_send, halo_recv, row_send, row_recv, col_send, col_recv,
+    rows, cols, x, out, u, df, prim, xr, xl, yt, yb, rxl, rxr, rya, ryb, rc, mine, others,
+    in_sem, halo_send, halo_recv, peak_send, peak_recv,
 ):
     ny, nx = x.shape[2], x.shape[3]
     me_r, me_c = lax.axis_index("row"), lax.axis_index("col")
@@ -98,11 +98,15 @@
     load.start()
 
     barrier = pltpu.get_barrier_semaphore()
-    peers = [(row_at(d), me_c) for d in range(1, rows)]
-    peers += [(me_r, col_at(d)) for d in range(1, cols)]
-    peers += [(row_at(a), col_at(b)) for a in (1, -1) for b in (1, -1)]
-    for peer in peers:
-        pl.semaphore_signal(barrier, inc=1, device_id=peer, device_id_type=MESH)
+    count = rows * cols
+
+    def peer(d):
+        return lax.rem(me_r + d // cols, rows), lax.rem(me_c + d % cols, cols)
+
+    @pl.loop(1, count)
+    def _(d):
+        pl.semaphore_signal(barrier, inc=1, device_id=peer(d), device_id_type=MESH)
+
     load.wait()
 
     peak = None
@@ -115,22 +119,7 @@
         for c in range(0, nx, LANES):
             part = speed[:, c : c + LANES]
             peak = part if peak is None else jnp.maximum(peak, part)
-    m0[...] = peak
-    pl.semaphore_wait(barrier, len(peers))
-
-    sends = []
-
-    def send(src, dst, send_sem, recv_sem, device):
-        copy = pltpu.make_async_remote_copy(
-            src_ref=src, dst_ref=dst, send_sem=send_sem, recv_sem=recv_sem,
-            device_id=device, device_id_type=MESH,
-        )
-        copy.start()
-        sends.append(copy)
-        return copy
-
-    for d in range(1, rows):
-        send(m0, m1.at[d - 1], row_send.at[d - 1], row_recv, (row_at(d), me_c))
+    mine[...] = jnp.max(peak, axis=0, keepdims=True)
 
     lane = lax.broadcasted_iota(jnp.int32, (ny, LANES), 1)
     pack_r = pack_l = None
@@ -150,6 +139,13 @@
         yb[3 * f : 3 * f + 3, :] = u[f, ny - 3 : ny, :]
     yt[15:16, :] = u[0, 0:1, :]
     yb[15:16, :] = u[0, 0:1, :]
+    up, down = shifts(nx, 1)
+    for r in range(0, ny, SUBLANES):
+        profiles = [prim[f, r : r + SUBLANES, :] for f in range(5)]
+        for f, difference in enumerate(flux_differences(profiles, up, down, 1)):
+            df[f, r : r + SUBLANES, :] = difference
+
+    pl.semaphore_wait(barrier, count - 1)
     top, bottom = pl.ds(0, SUBLANES), pl.ds(ny - SUBLANES, SUBLANES)
     halos = []
     for i, (src, dst, device) in enumerate(
@@ -164,21 +160,21 @@
             (xl.at[top], rc.at[3], (row_at(-1), col_at(-1))),
         ]
     ):
-        halos.append(send(src, dst, halo_send.at[i], halo_recv.at[i], device))
-
-    pltpu.make_async_copy(m1, m1, row_recv).wait()
-    peak = m0[...]
-    for d in range(rows - 1):
-        peak = jnp.maximum(peak, m1[d])
-    m1s[...] = peak
-    for d in range(1, cols):
-        send(m1s, m2.at[d - 1], col_send.at[d - 1], col_recv, (me_r, col_at(d)))
-
-    up, down = shifts(nx, 1)
-    for r in range(0, ny, SUBLANES):
-        profiles = [prim[f, r : r + SUBLANES, :] for f in range(5)]
-        for f, difference in enumerate(flux_differences(profiles, up, down, 1)):
-            df[f, r : r + SUBLANES, :] = difference
+        halos.append(
+            pltpu.make_async_remote_copy(
+                src_ref=src, dst_ref=dst, send_sem=halo_send.at[i], recv_sem=halo_recv.at[i],
+                device_id=device, device_id_type=MESH,
+            )
+        )
+        halos[i].start()
+
+
+    @pl.loop(1, count)
+    def _(d):
+        pltpu.make_async_remote_copy(
+            src_ref=mine, dst_ref=others.at[d - 1], send_sem=peak_send, recv_sem=peak_recv,
+            device_id=peer(d), device_id_type=MESH,
+        ).start()
 
     halos[0].wait_recv()
     halos[1].wait_recv()
@@ -214,10 +210,9 @@
             lane >= 125, pltpu.roll(difference, 64, 1), df[f, :, nx - LANES : nx]
         )
 
-    pltpu.make_async_copy(m2, m2, col_recv).wait()
-    for d in range(cols - 1):
-        peak = jnp.maximum(peak, m2[d])
-    peak = jnp.max(jnp.max(peak, axis=0, keepdims=True), axis=1, keepdims=True)
+    pltpu.make_async_copy(others, others, peak_recv).wait()
+    peak = jnp.maximum(mine[...], jnp.max(others[...], axis=0))
+    peak = jnp.max(peak, axis=1, keepdims=True)
     half_step = (0.5 * COURANT) / peak
 
     up, down = shifts(total, 0)
@@ -230,8 +225,9 @@
             result = cells[f] - half_step * difference
             out[f, 0, :, c : c + LANES] = result[0:ny]
 
-    for copy in sends:
+    for copy in halos:
         copy.wait_send()
+    pltpu.make_async_copy(others, others, peak_send).wait()
 
 
 def local(rows, cols, fields):
@@ -241,7 +237,7 @@
     return pl.pallas_call(
         functools.partial(kernel, rows, cols),
         out_shape=jax.ShapeDtypeStruct(fields.shape, fields.dtype),
-        in_specs=[pl.BlockSpec(memory_space=pl.ANY)],
+        in_specs=[pl.BlockSpec(memory_space=pltpu.HBM)],
         out_specs=pl.BlockSpec(memory_space=pltpu.VMEM),
         scratch_shapes=[
             vmem(5, ny + SUBLANES, nx),
@@ -256,16 +252,12 @@
             vmem(16, nx),
             vmem(16, nx),
             vmem(4, SUBLANES, LANES),
-            vmem(SUBLANES, LANES),
-            vmem(rows - 1, SUBLANES, LANES),
-            vmem(SUBLANES, LANES),
-            vmem(cols - 1, SUBLANES, LANES),
+            vmem(1, LANES),
+            vmem(rows * cols - 1, 1, LANES),
             dma,
             dma((8,)),
             dma((8,)),
-            dma((rows - 1,)),
             dma,
-            dma((cols - 1,)),
             dma,
         ],
         compiler_params=pltpu.CompilerParams(

time: 14.5 us -> 12.8 us (0.88)
  Pallas kernels: 12.8 us -> 11.1 us
    pallas_call x1, Pallas kernels: 12.8 us -> 11.1 us  [local(): pl.pallas_call(functools.partial(kernel, rows, cols), out_shape=jax.Shape...]
where the time goes in v2:
time: 12.8 us; the launch traced here: 12.7 us
  Pallas kernels  11.1 us (87%)
  local copies, waits for them, and re-layouts  1.58 us (12%)
    pallas_call x1, Pallas kernels, local(): pl.pallas_call(functools.partial(kernel, rows, cols), out_shape=jax.Shape...  11.1 us
    unnamed x3, local copies, waits for them, and re-layouts  1.58 us

profile of v2, /device:TPU:0, one launch (start us, length us, event | category | flops | bytes accessed | tf_op | source)
XLA Modules:
  0.0 12.7 jit_solution(16297901317324583690)
XLA Ops:
  0.0 0.0 copy-start
  0.0 0.9 %copy-done = f32[5,1,16,512]{3,2,1,0:T(8,128)S(1)} copy-done((f32[5,1,16,512]{3,2,1,0:T(8,128)S(1)}, f32[5,1,16,512]{3,2,1,0:T(8,128)}, u32[]{:S(2)}) %copy-start) | copy-done | bytes 163864
  0.9 11.1 %sweeps.1 = f32[5,1,16,512]{3,2,1,0:T(8,128)S(1)} custom-call(f32[5,1,16,512]{3,2,1,0:T(8,128)S(1)} %copy-done), custom_call_target="tpu_custom_call" | custom-call | tf_op jit(solution)/shard_map/sweeps/pallas_call | solution.py:237
  12.0 0.7 %copy.3 = f32[5,1,16,512]{3,2,1,0:T(8,128)} copy(f32[5,1,16,512]{3,2,1,0:T(8,128)S(1)} %sweeps.1) | data formatting | bytes 327680
Async XLA Ops:
  0.0 0.9 %copy-start = (f32[5,1,16,512]{3,2,1,0:T(8,128)S(1)}, f32[5,1,16,512]{3,2,1,0:T(8,128)}, u32[]{:S(2)}) copy-start(f32[5,1,16,512]{3,2,1,0:T(8,128)} %x.1) | copy-start | bytes 491524

commit v3 on v2

--- a/solution.py
+++ b/solution.py
@@ -13,6 +13,7 @@
 LANES = 128
 SUBLANES = 8
 TINY = 1e-37
+UNROLLED = 64
 
 
 def inverse(value):
@@ -100,12 +101,22 @@
     barrier = pltpu.get_barrier_semaphore()
     count = rows * cols
 
-    def peer(d):
-        return lax.rem(me_r + d // cols, rows), lax.rem(me_c + d % cols, cols)
-
-    @pl.loop(1, count)
-    def _(d):
-        pl.semaphore_signal(barrier, inc=1, device_id=peer(d), device_id_type=MESH)
+    def for_peers(act):
+        if count <= UNROLLED:
+            at_row = [row_at(a) for a in range(rows)]
+            at_col = [col_at(b) for b in range(cols)]
+            for d in range(1, count):
+                act(d, (at_row[d // cols], at_col[d % cols]))
+        else:
+
+            @pl.loop(1, count)
+            def _(d):
+                act(d, (lax.rem(me_r + d // cols, rows), lax.rem(me_c + d % cols, cols)))
+
+    def greet(d, peer):
+        pl.semaphore_signal(barrier, inc=1, device_id=peer, device_id_type=MESH)
+
+    for_peers(greet)
 
     load.wait()
 
@@ -139,12 +150,6 @@
         yb[3 * f : 3 * f + 3, :] = u[f, ny - 3 : ny, :]
     yt[15:16, :] = u[0, 0:1, :]
     yb[15:16, :] = u[0, 0:1, :]
-    up, down = shifts(nx, 1)
-    for r in range(0, ny, SUBLANES):
-        profiles = [prim[f, r : r + SUBLANES, :] for f in range(5)]
-        for f, difference in enumerate(flux_differences(profiles, up, down, 1)):
-            df[f, r : r + SUBLANES, :] = difference
-
     pl.semaphore_wait(barrier, count - 1)
     top, bottom = pl.ds(0, SUBLANES), pl.ds(ny - SUBLANES, SUBLANES)
     halos = []
@@ -168,13 +173,19 @@
         )
         halos[i].start()
 
-
-    @pl.loop(1, count)
-    def _(d):
+    def tell(d, peer):
         pltpu.make_async_remote_copy(
             src_ref=mine, dst_ref=others.at[d - 1], send_sem=peak_send, recv_sem=peak_recv,
-            device_id=peer(d), device_id_type=MESH,
+            device_id=peer, device_id_type=MESH,
         ).start()
+
+    for_peers(tell)
+
+    up, down = shifts(nx, 1)
+    for r in range(0, ny, SUBLANES):
+        profiles = [prim[f, r : r + SUBLANES, :] for f in range(5)]
+        for f, difference in enumerate(flux_differences(profiles, up, down, 1)):
+            df[f, r : r + SUBLANES, :] = difference
 
     halos[0].wait_recv()
     halos[1].wait_recv()
@@ -261,7 +272,7 @@
             dma,
         ],
         compiler_params=pltpu.CompilerParams(
-            collective_id=0, has_side_effects=True, vmem_limit_bytes=32 * 1024 * 1024
+            collective_id=0, has_side_effects=True, vmem_limit_bytes=55072 * 1024
         ),
         name="sweeps",
     )(fields)

time: 12.8 us -> 11.8 us (0.922)
  the two profiles are of different devices: /device:TPU:0 before, /device:TPU:1 now
where the time goes in v3:
time: 11.8 us; the launch traced here: 11.7 us
  Pallas kernels  11 us (93%)
  local copies, waits for them, and re-layouts  0.67 us (6%)
    pallas_call x1, Pallas kernels, local(): pl.pallas_call(functools.partial(kernel, rows, cols), out_shape=jax.Shape...  11 us
    unnamed x1, local copies, waits for them, and re-layouts  0.67 us

profile of v3, /device:TPU:1, one launch (start us, length us, event | category | flops | bytes accessed | tf_op | source)
XLA Modules:
  0.0 11.7 jit_solution(6952741270080279257)
XLA Ops:
  0.0 11.0 %sweeps.1 = f32[5,1,16,512]{3,2,1,0:T(8,128)S(1)} custom-call(f32[5,1,16,512]{3,2,1,0:T(8,128)} %x.1), custom_call_target="tpu_custom_call" | custom-call | tf_op jit(solution)/shard_map/sweeps/pallas_call | solution.py:248
  11.0 0.7 %copy.3 = f32[5,1,16,512]{3,2,1,0:T(8,128)} copy(f32[5,1,16,512]{3,2,1,0:T(8,128)S(1)} %sweeps.1) | data formatting | bytes 327680

commit v4 on v3

--- a/solution.py
+++ b/solution.py
@@ -40,22 +40,23 @@
 
 def face_values(q, up, down):
     after = up(q)
-    edge = 7.0 / 12.0 * (q + after) - 1.0 / 12.0 * (down(q) + up(after))
-    edge = jnp.minimum(jnp.maximum(edge, jnp.minimum(q, after)), jnp.maximum(q, after))
-    rise = edge - q
-    fall = q - down(edge)
+    jump = after - q
+    rise = 0.5 * jump + (1.0 / 12.0) * (down(jump) - up(jump))
+    rise = jnp.minimum(jnp.maximum(rise, jnp.minimum(jump, 0.0)), jnp.maximum(jump, 0.0))
+    next_fall = jump - rise
+    fall, next_rise = down(next_fall), up(rise)
     right = q + limited(rise, fall + fall)
-    left = q - limited(fall, rise + rise)
-    return right, up(left)
+    next_left = after - limited(next_fall, next_rise + next_rise)
+    return right, next_left
 
 
 def face_terms(state, normal):
     density, pressure = state[0], state[4]
     velocity = state[1:4]
-    square = velocity[0] * velocity[0] + velocity[1] * velocity[1] + velocity[2] * velocity[2]
-    energy = pressure * (1.0 / (GAMMA - 1.0)) + 0.5 * density * square
+    momentum = [density * v for v in velocity]
+    square = momentum[0] * velocity[0] + momentum[1] * velocity[1] + momentum[2] * velocity[2]
+    energy = pressure * (1.0 / (GAMMA - 1.0)) + 0.5 * square
     speed = velocity[normal - 1]
-    momentum = [density * v for v in velocity]
     mass_flux = momentum[normal - 1]
     flux = [mass_flux] + [mass_flux * v for v in velocity] + [speed * (energy + pressure)]
     flux[normal] = flux[normal] + pressure

time: 11.8 us -> 11.7 us (level)
  the two profiles are of different devices: /device:TPU:1 before, /device:TPU:0 now
where the time goes in v4:
time: 11.7 us; the launch traced here: 11.5 us
  Pallas kernels  10.8 us (92%)
  local copies, waits for them, and re-layouts  0.67 us (6%)
    pallas_call x1, Pallas kernels, local(): pl.pallas_call(functools.partial(kernel, rows, cols), out_shape=jax.Shape...  10.8 us
    unnamed x1, local copies, waits for them, and re-layouts  0.67 us

profile of v4, /device:TPU:0, one launch (start us, length us, event | category | flops | bytes accessed | tf_op | source)
XLA Modules:
  0.0 11.5 jit_solution(10073565527158602814)
XLA Ops:
  0.0 10.8 %sweeps.1 = f32[5,1,16,512]{3,2,1,0:T(8,128)S(1)} custom-call(f32[5,1,16,512]{3,2,1,0:T(8,128)} %x.1), custom_call_target="tpu_custom_call" | custom-call | tf_op jit(solution)/shard_map/sweeps/pallas_call | solution.py:249
  10.8 0.7 %copy.3 = f32[5,1,16,512]{3,2,1,0:T(8,128)} copy(f32[5,1,16,512]{3,2,1,0:T(8,128)S(1)} %sweeps.1) | data formatting | bytes 327680

commit v5 on v4

--- a/solution.py
+++ b/solution.py
@@ -84,7 +84,7 @@
 
 
 def kernel(
-    rows, cols, x, out, u, df, prim, xr, xl, yt, yb, rxl, rxr, rya, ryb, rc, mine, others,
+    rows, cols, x, out, u, df, xr, xl, yt, yb, rxl, rxr, rya, ryb, rc, mine, others,
     in_sem, halo_send, halo_recv, peak_send, peak_recv,
 ):
     ny, nx = x.shape[2], x.shape[3]
@@ -124,8 +124,6 @@
     peak = None
     for r in range(0, ny, SUBLANES):
         profiles, inverse_density = primitives([u[f, r : r + SUBLANES, :] for f in range(5)])
-        for f in range(5):
-            prim[f, r : r + SUBLANES, :] = profiles[f]
         speed = jnp.maximum(jnp.abs(profiles[1]), jnp.abs(profiles[2]))
         speed = speed + root(GAMMA * profiles[4] * inverse_density)
         for c in range(0, nx, LANES):
@@ -183,20 +181,22 @@
     for_peers(tell)
 
     up, down = shifts(nx, 1)
-    for r in range(0, ny, SUBLANES):
-        profiles = [prim[f, r : r + SUBLANES, :] for f in range(5)]
+
+    @pl.loop(0, ny // SUBLANES + 1)
+    def _(tile):
+        @pl.when(tile == ny // SUBLANES)
+        def _():
+            halos[0].wait_recv()
+            halos[1].wait_recv()
+            for f in range(5):
+                u[f, ny : ny + 3, :] = ryb[3 * f : 3 * f + 3, :]
+                u[f, ny + 3 : ny + 5, :] = u[f, 3:5, :]
+                u[f, ny + 5 : ny + 8, :] = rya[3 * f : 3 * f + 3, :]
+
+        at = pl.ds(pl.multiple_of(tile * SUBLANES, SUBLANES), SUBLANES)
+        profiles, _ = primitives([u[f, at, :] for f in range(5)])
         for f, difference in enumerate(flux_differences(profiles, up, down, 1)):
-            df[f, r : r + SUBLANES, :] = difference
-
-    halos[0].wait_recv()
-    halos[1].wait_recv()
-    for f in range(5):
-        u[f, ny : ny + 3, :] = ryb[3 * f : 3 * f + 3, :]
-        u[f, ny + 3 : ny + 5, :] = u[f, 3:5, :]
-        u[f, ny + 5 : ny + 8, :] = rya[3 * f : 3 * f + 3, :]
-    profiles, _ = primitives([u[f, ny : ny + SUBLANES, :] for f in range(5)])
-    for f, difference in enumerate(flux_differences(profiles, up, down, 1)):
-        df[f, ny : ny + SUBLANES, :] = difference
+            df[f, at, :] = difference
 
     for copy in halos[2:]:
         copy.wait_recv()
@@ -228,14 +228,15 @@
     half_step = (0.5 * COURANT) / peak
 
     up, down = shifts(total, 0)
-    for c in range(0, nx, LANES):
-        cells = [
-            u[f, :, c : c + LANES] - half_step * df[f, :, c : c + LANES] for f in range(5)
-        ]
+
+    @pl.loop(0, nx // LANES)
+    def _(chunk):
+        at = pl.ds(pl.multiple_of(chunk * LANES, LANES), LANES)
+        cells = [u[f, :, at] - half_step * df[f, :, at] for f in range(5)]
         profiles, _ = primitives(cells)
         for f, difference in enumerate(flux_differences(profiles, up, down, 2)):
             result = cells[f] - half_step * difference
-            out[f, 0, :, c : c + LANES] = result[0:ny]
+            out[f, 0, :, at] = result[0:ny]
 
     for copy in halos:
         copy.wait_send()
@@ -254,7 +255,6 @@
         scratch_shapes=[
             vmem(5, ny + SUBLANES, nx),
             vmem(5, ny + SUBLANES, nx),
-            vmem(5, ny, nx),
             vmem(ny, LANES),
             vmem(ny, LANES),
             vmem(16, nx),

time: 11.7 us -> 11.6 us (level)
  no operation moved by 1% of the time
where the time goes in v5:
time: 11.6 us; the launch traced here: 11.4 us
  Pallas kernels  10.7 us (92%)
  local copies, waits for them, and re-layouts  0.67 us (6%)
    pallas_call x1, Pallas kernels, local(): pl.pallas_call(functools.partial(kernel, rows, cols), out_shape=jax.Shape...  10.7 us
    unnamed x1, local copies, waits for them, and re-layouts  0.67 us

profile of v5, /device:TPU:0, one launch (start us, length us, event | category | flops | bytes accessed | tf_op | source)
XLA Modules:
  0.0 11.4 jit_solution(8471591897180228760)
XLA Ops:
  0.0 10.7 %sweeps.1 = f32[5,1,16,512]{3,2,1,0:T(8,128)S(1)} custom-call(f32[5,1,16,512]{3,2,1,0:T(8,128)} %x.1), custom_call_target="tpu_custom_call" | custom-call | tf_op jit(solution)/shard_map/sweeps/pallas_call | solution.py:250
  10.7 0.7 %copy.3 = f32[5,1,16,512]{3,2,1,0:T(8,128)} copy(f32[5,1,16,512]{3,2,1,0:T(8,128)S(1)} %sweeps.1) | data formatting | bytes 327680

commit v6 on v5

--- a/solution.py
+++ b/solution.py
@@ -84,8 +84,8 @@
 
 
 def kernel(
-    rows, cols, x, out, u, df, xr, xl, yt, yb, rxl, rxr, rya, ryb, rc, mine, others,
-    in_sem, halo_send, halo_recv, peak_send, peak_recv,
+    rows, cols, x, out, u, df, xr, xl, yt, yb, rxl, rxr, rya, ryb, rc, mine, theirs, both, others,
+    in_sem, halo_send, halo_recv, pair_send, pair_recv, peak_send, peak_recv,
 ):
     ny, nx = x.shape[2], x.shape[3]
     me_r, me_c = lax.axis_index("row"), lax.axis_index("col")
@@ -100,25 +100,31 @@
     load.start()
 
     barrier = pltpu.get_barrier_semaphore()
-    count = rows * cols
-
-    def for_peers(act):
+    partner = (me_r, me_c + 1 - 2 * lax.rem(me_c, 2))
+    half = cols // 2
+    count = rows * half
+
+    def for_chips(act):
         if count <= UNROLLED:
             at_row = [row_at(a) for a in range(rows)]
-            at_col = [col_at(b) for b in range(cols)]
+            at_col = [col_at(2 * b) for b in range(half)]
             for d in range(1, count):
-                act(d, (at_row[d // cols], at_col[d % cols]))
+                act(d, (at_row[d // half], at_col[d % half]))
         else:
 
             @pl.loop(1, count)
             def _(d):
-                act(d, (lax.rem(me_r + d // cols, rows), lax.rem(me_c + d % cols, cols)))
+                step = 2 * (d % half)
+                act(d, (lax.rem(me_r + d // half, rows), lax.rem(me_c + step, cols)))
 
     def greet(d, peer):
         pl.semaphore_signal(barrier, inc=1, device_id=peer, device_id_type=MESH)
 
-    for_peers(greet)
-
+    near = [(me_r, col_at(b)) for b in (1, -1)]
+    near += [(row_at(a), col_at(b)) for a in (1, -1) for b in (1, -1)]
+    for peer in near:
+        greet(0, peer)
+    for_chips(greet)
     load.wait()
 
     peak = None
@@ -149,7 +155,12 @@
         yb[3 * f : 3 * f + 3, :] = u[f, ny - 3 : ny, :]
     yt[15:16, :] = u[0, 0:1, :]
     yb[15:16, :] = u[0, 0:1, :]
-    pl.semaphore_wait(barrier, count - 1)
+    pl.semaphore_wait(barrier, count - 1 + len(near))
+    pair = pltpu.make_async_remote_copy(
+        src_ref=mine, dst_ref=theirs, send_sem=pair_send, recv_sem=pair_recv,
+        device_id=partner, device_id_type=MESH,
+    )
+    pair.start()
     top, bottom = pl.ds(0, SUBLANES), pl.ds(ny - SUBLANES, SUBLANES)
     halos = []
     for i, (src, dst, device) in enumerate(
@@ -172,34 +183,36 @@
         )
         halos[i].start()
 
+    pair.wait_recv()
+    both[...] = jnp.maximum(mine[...], theirs[...])
+
     def tell(d, peer):
         pltpu.make_async_remote_copy(
-            src_ref=mine, dst_ref=others.at[d - 1], send_sem=peak_send, recv_sem=peak_recv,
+            src_ref=both, dst_ref=others.at[d - 1], send_sem=peak_send, recv_sem=peak_recv,
             device_id=peer, device_id_type=MESH,
         ).start()
 
-    for_peers(tell)
+    for_chips(tell)
 
     up, down = shifts(nx, 1)
 
-    @pl.loop(0, ny // SUBLANES + 1)
-    def _(tile):
-        @pl.when(tile == ny // SUBLANES)
-        def _():
-            halos[0].wait_recv()
-            halos[1].wait_recv()
-            for f in range(5):
-                u[f, ny : ny + 3, :] = ryb[3 * f : 3 * f + 3, :]
-                u[f, ny + 3 : ny + 5, :] = u[f, 3:5, :]
-                u[f, ny + 5 : ny + 8, :] = rya[3 * f : 3 * f + 3, :]
-
-        at = pl.ds(pl.multiple_of(tile * SUBLANES, SUBLANES), SUBLANES)
+    def sweep_tile(at):
         profiles, _ = primitives([u[f, at, :] for f in range(5)])
         for f, difference in enumerate(flux_differences(profiles, up, down, 1)):
             df[f, at, :] = difference
 
-    for copy in halos[2:]:
+    @pl.loop(0, ny // SUBLANES)
+    def _(tile):
+        sweep_tile(pl.ds(pl.multiple_of(tile * SUBLANES, SUBLANES), SUBLANES))
+
+    for copy in halos:
         copy.wait_recv()
+    for f in range(5):
+        u[f, ny : ny + 3, :] = ryb[3 * f : 3 * f + 3, :]
+        u[f, ny + 3 : ny + 5, :] = u[f, 3:5, :]
+        u[f, ny + 5 : ny + 8, :] = rya[3 * f : 3 * f + 3, :]
+    sweep_tile(pl.ds(ny, SUBLANES))
+
     total = ny + SUBLANES
     lane = lax.broadcasted_iota(jnp.int32, (total, LANES), 1)
     below = lax.broadcasted_iota(jnp.int32, (SUBLANES, LANES), 0) < 4
@@ -223,7 +236,7 @@
         )
 
     pltpu.make_async_copy(others, others, peak_recv).wait()
-    peak = jnp.maximum(mine[...], jnp.max(others[...], axis=0))
+    peak = jnp.maximum(both[...], jnp.max(others[...], axis=0))
     peak = jnp.max(peak, axis=1, keepdims=True)
     half_step = (0.5 * COURANT) / peak
 
@@ -240,6 +253,7 @@
 
     for copy in halos:
         copy.wait_send()
+    pair.wait_send()
     pltpu.make_async_copy(others, others, peak_send).wait()
 
 
@@ -265,10 +279,14 @@
             vmem(16, nx),
             vmem(4, SUBLANES, LANES),
             vmem(1, LANES),
-            vmem(rows * cols - 1, 1, LANES),
+            vmem(1, LANES),
+            vmem(1, LANES),
+            vmem(rows * cols // 2 - 1, 1, LANES),
             dma,
             dma((8,)),
             dma((8,)),
+            dma,
+            dma,
             dma,
             dma,
         ],

time: 11.6 us -> 11.6 us (level)
  no operation moved by 1% of the time
where the time goes in v6:
time: 11.6 us; the launch traced here: 11.5 us
  Pallas kernels  10.8 us (93%)
  local copies, waits for them, and re-layouts  0.67 us (6%)
    pallas_call x1, Pallas kernels, local(): pl.pallas_call(functools.partial(kernel, rows, cols), out_shape=jax.Shape...  10.8 us
    unnamed x1, local copies, waits for them, and re-layouts  0.67 us

profile of v6, /device:TPU:0, one launch (start us, length us, event | category | flops | bytes accessed | tf_op | source)
XLA Modules:
  0.0 11.5 jit_solution(814359978637700732)
XLA Ops:
  0.0 10.8 %sweeps.1 = f32[5,1,16,512]{3,2,1,0:T(8,128)S(1)} custom-call(f32[5,1,16,512]{3,2,1,0:T(8,128)} %x.1), custom_call_target="tpu_custom_call" | custom-call | tf_op jit(solution)/shard_map/sweeps/pallas_call | solution.py:264
  10.8 0.7 %copy.3 = f32[5,1,16,512]{3,2,1,0:T(8,128)} copy(f32[5,1,16,512]{3,2,1,0:T(8,128)S(1)} %sweeps.1) | data formatting | bytes 327680

commit v7 on v6

--- a/solution.py
+++ b/solution.py
@@ -16,22 +16,18 @@
 UNROLLED = 64
 
 
-def inverse(value):
-    guess = pl.reciprocal(value, approx=True)
-    return guess * (2.0 - value * guess)
-
-
-def root(value):
-    return value * lax.rsqrt(jnp.maximum(value, TINY))
+def sound(density, pressure):
+    scaled = GAMMA * pressure
+    return scaled * lax.rsqrt(jnp.maximum(scaled, TINY)) * lax.rsqrt(density)
 
 
 def primitives(cells):
     density = cells[0]
-    inverse_density = inverse(density)
+    inverse_density = pl.reciprocal(density, approx=True)
     velocity = [cells[k] * inverse_density for k in (1, 2, 3)]
     square = velocity[0] * velocity[0] + velocity[1] * velocity[1] + velocity[2] * velocity[2]
     pressure = (GAMMA - 1.0) * (cells[4] - 0.5 * density * square)
-    return [density] + velocity + [pressure], inverse_density
+    return [density] + velocity + [pressure]
 
 
 def limited(first, second):
@@ -50,30 +46,28 @@
     return right, next_left
 
 
-def face_terms(state, normal):
-    density, pressure = state[0], state[4]
-    velocity = state[1:4]
-    momentum = [density * v for v in velocity]
-    square = momentum[0] * velocity[0] + momentum[1] * velocity[1] + momentum[2] * velocity[2]
-    energy = pressure * (1.0 / (GAMMA - 1.0)) + 0.5 * square
-    speed = velocity[normal - 1]
-    mass_flux = momentum[normal - 1]
-    flux = [mass_flux] + [mass_flux * v for v in velocity] + [speed * (energy + pressure)]
-    flux[normal] = flux[normal] + pressure
-    signal = jnp.abs(speed) + root(GAMMA * pressure * inverse(density))
-    return [density] + momentum + [energy], flux, signal
-
-
 def flux_differences(profiles, up, down, normal):
     pairs = [face_values(q, up, down) for q in profiles]
-    left_cons, left_flux, left_signal = face_terms([a for a, _ in pairs], normal)
-    right_cons, right_flux, right_signal = face_terms([b for _, b in pairs], normal)
-    signal = jnp.maximum(left_signal, right_signal)
-    results = []
-    for k in range(5):
-        flux = (left_flux[k] + right_flux[k]) - signal * (right_cons[k] - left_cons[k])
-        results.append(flux - down(flux))
-    return results
+    sides = [[pair[side] for pair in pairs] for side in range(2)]
+    signal = None
+    for density, pressure, speed in [(side[0], side[4], side[normal]) for side in sides]:
+        own = jnp.abs(speed) + sound(density, pressure)
+        signal = own if signal is None else jnp.maximum(signal, own)
+    shifted = [sides[0][normal] + signal, sides[1][normal] - signal]
+    mass = [side[0] * speed for side, speed in zip(sides, shifted)]
+    fluxes = [mass[0] + mass[1]]
+    kinetic = None
+    for k in (1, 2, 3):
+        left, right = mass[0] * sides[0][k], mass[1] * sides[1][k]
+        work = left * sides[0][k] + right * sides[1][k]
+        kinetic = work if kinetic is None else kinetic + work
+        fluxes.append(left + right)
+    fluxes[normal] = fluxes[normal] + (sides[0][4] + sides[1][4])
+    energy = 0.5 * kinetic
+    for side, speed in zip(sides, shifted):
+        energy = energy + side[4] * (speed * (1.0 / (GAMMA - 1.0)) + side[normal])
+    fluxes.append(energy)
+    return [flux - down(flux) for flux in fluxes]
 
 
 def shifts(length, axis):
@@ -129,9 +123,9 @@
 
     peak = None
     for r in range(0, ny, SUBLANES):
-        profiles, inverse_density = primitives([u[f, r : r + SUBLANES, :] for f in range(5)])
+        profiles = primitives([u[f, r : r + SUBLANES, :] for f in range(5)])
         speed = jnp.maximum(jnp.abs(profiles[1]), jnp.abs(profiles[2]))
-        speed = speed + root(GAMMA * profiles[4] * inverse_density)
+        speed = speed + sound(profiles[0], profiles[4])
         for c in range(0, nx, LANES):
             part = speed[:, c : c + LANES]
             peak = part if peak is None else jnp.maximum(peak, part)
@@ -197,7 +191,7 @@
     up, down = shifts(nx, 1)
 
     def sweep_tile(at):
-        profiles, _ = primitives([u[f, at, :] for f in range(5)])
+        profiles = primitives([u[f, at, :] for f in range(5)])
         for f, difference in enumerate(flux_differences(profiles, up, down, 1)):
             df[f, at, :] = difference
 
@@ -227,7 +221,7 @@
         tile = jnp.where(lane < 32, begin, end)
         tile = jnp.where(lane >= 125, before, tile)
         seam.append(jnp.where((lane >= 64) & (lane < 67), after, tile))
-    profiles, _ = primitives(seam)
+    profiles = primitives(seam)
     up, down = shifts(LANES, 1)
     for f, difference in enumerate(flux_differences(profiles, up, down, 1)):
         df[f, :, 0:LANES] = jnp.where(lane < 3, difference, df[f, :, 0:LANES])
@@ -246,7 +240,7 @@
     def _(chunk):
         at = pl.ds(pl.multiple_of(chunk * LANES, LANES), LANES)
         cells = [u[f, :, at] - half_step * df[f, :, at] for f in range(5)]
-        profiles, _ = primitives(cells)
+        profiles = primitives(cells)
         for f, difference in enumerate(flux_differences(profiles, up, down, 2)):
             result = cells[f] - half_step * difference
             out[f, 0, :, at] = result[0:ny]

time: 11.6 us -> 11.6 us (level)
  no operation moved by 1% of the time
where the time goes in v7:
time: 11.6 us; the launch traced here: 11.4 us
  Pallas kernels  10.8 us (93%)
  local copies, waits for them, and re-layouts  0.67 us (6%)
    pallas_call x1, Pallas kernels, local(): pl.pallas_call(functools.partial(kernel, rows, cols), out_shape=jax.Shape...  10.8 us
    unnamed x1, local copies, waits for them, and re-layouts  0.67 us

profile of v7, /device:TPU:0, one launch (start us, length us, event | category | flops | bytes accessed | tf_op | source)
XLA Modules:
  0.0 11.4 jit_solution(10011144682185736963)
XLA Ops:
  0.0 10.8 %sweeps.1 = f32[5,1,16,512]{3,2,1,0:T(8,128)S(1)} custom-call(f32[5,1,16,512]{3,2,1,0:T(8,128)} %x.1), custom_call_target="tpu_custom_call" | custom-call | tf_op jit(solution)/shard_map/sweeps/pallas_call | solution.py:258
  10.8 0.7 %copy.3 = f32[5,1,16,512]{3,2,1,0:T(8,128)} copy(f32[5,1,16,512]{3,2,1,0:T(8,128)S(1)} %sweeps.1) | data formatting | bytes 327680

commit v8 on v7

--- a/solution.py
+++ b/solution.py
@@ -195,9 +195,11 @@
         for f, difference in enumerate(flux_differences(profiles, up, down, 1)):
             df[f, at, :] = difference
 
-    @pl.loop(0, ny // SUBLANES)
+    deep = 2 * SUBLANES if ny % (2 * SUBLANES) == 0 else SUBLANES
+
+    @pl.loop(0, ny // deep)
     def _(tile):
-        sweep_tile(pl.ds(pl.multiple_of(tile * SUBLANES, SUBLANES), SUBLANES))
+        sweep_tile(pl.ds(pl.multiple_of(tile * deep, deep), deep))
 
     for copy in halos:
         copy.wait_recv()
@@ -236,9 +238,11 @@
 
     up, down = shifts(total, 0)
 
-    @pl.loop(0, nx // LANES)
+    wide = 2 * LANES if nx % (2 * LANES) == 0 else LANES
+
+    @pl.loop(0, nx // wide)
     def _(chunk):
-        at = pl.ds(pl.multiple_of(chunk * LANES, LANES), LANES)
+        at = pl.ds(pl.multiple_of(chunk * wide, wide), wide)
         cells = [u[f, :, at] - half_step * df[f, :, at] for f in range(5)]
         profiles = primitives(cells)
         for f, difference in enumerate(flux_differences(profiles, up, down, 2)):

time: 11.6 us -> 11.6 us (level)
  no operation moved by 1% of the time
where the time goes in v8:
time: 11.6 us; the launch traced here: 11.4 us
  Pallas kernels  10.7 us (92%)
  local copies, waits for them, and re-layouts  0.67 us (6%)
    pallas_call x1, Pallas kernels, local(): pl.pallas_call(functools.partial(kernel, rows, cols), out_shape=jax.Shape...  10.7 us
    unnamed x1, local copies, waits for them, and re-layouts  0.67 us

profile of v8, /device:TPU:0, one launch (start us, length us, event | category | flops | bytes accessed | tf_op | source)
XLA Modules:
  0.0 11.4 jit_solution(10668525878960854149)
XLA Ops:
  0.0 10.7 %sweeps.1 = f32[5,1,16,512]{3,2,1,0:T(8,128)S(1)} custom-call(f32[5,1,16,512]{3,2,1,0:T(8,128)} %x.1), custom_call_target="tpu_custom_call" | custom-call | tf_op jit(solution)/shard_map/sweeps/pallas_call | solution.py:262
  10.8 0.7 %copy.3 = f32[5,1,16,512]{3,2,1,0:T(8,128)} copy(f32[5,1,16,512]{3,2,1,0:T(8,128)S(1)} %sweeps.1) | data formatting | bytes 327680

commit v9 on v8

--- a/solution.py
+++ b/solution.py
@@ -131,6 +131,13 @@
             peak = part if peak is None else jnp.maximum(peak, part)
     mine[...] = jnp.max(peak, axis=0, keepdims=True)
 
+    pl.semaphore_wait(barrier, count - 1 + len(near))
+    pair = pltpu.make_async_remote_copy(
+        src_ref=mine, dst_ref=theirs, send_sem=pair_send, recv_sem=pair_recv,
+        device_id=partner, device_id_type=MESH,
+    )
+    pair.start()
+
     lane = lax.broadcasted_iota(jnp.int32, (ny, LANES), 1)
     pack_r = pack_l = None
     for f in range(5):
@@ -149,12 +156,6 @@
         yb[3 * f : 3 * f + 3, :] = u[f, ny - 3 : ny, :]
     yt[15:16, :] = u[0, 0:1, :]
     yb[15:16, :] = u[0, 0:1, :]
-    pl.semaphore_wait(barrier, count - 1 + len(near))
-    pair = pltpu.make_async_remote_copy(
-        src_ref=mine, dst_ref=theirs, send_sem=pair_send, recv_sem=pair_recv,
-        device_id=partner, device_id_type=MESH,
-    )
-    pair.start()
     top, bottom = pl.ds(0, SUBLANES), pl.ds(ny - SUBLANES, SUBLANES)
     halos = []
     for i, (src, dst, device) in enumerate(

time: 11.6 us -> 11.6 us (level)
  no operation moved by 1% of the time
where the time goes in v9:
time: 11.6 us; the launch traced here: 11.5 us
  Pallas kernels  10.8 us (93%)
  local copies, waits for them, and re-layouts  0.67 us (6%)
    pallas_call x1, Pallas kernels, local(): pl.pallas_call(functools.partial(kernel, rows, cols), out_shape=jax.Shape...  10.8 us
    unnamed x1, local copies, waits for them, and re-layouts  0.67 us

profile of v9, /device:TPU:0, one launch (start us, length us, event | category | flops | bytes accessed | tf_op | source)
XLA Modules:
  0.0 11.5 jit_solution(14502679708227340845)
XLA Ops:
  0.0 10.8 %sweeps.1 = f32[5,1,16,512]{3,2,1,0:T(8,128)S(1)} custom-call(f32[5,1,16,512]{3,2,1,0:T(8,128)} %x.1), custom_call_target="tpu_custom_call" | custom-call | tf_op jit(solution)/shard_map/sweeps/pallas_call | solution.py:263
  10.8 0.7 %copy.3 = f32[5,1,16,512]{3,2,1,0:T(8,128)} copy(f32[5,1,16,512]{3,2,1,0:T(8,128)S(1)} %sweeps.1) | data formatting | bytes 327680

commit v10 on v8

--- a/solution.py
+++ b/solution.py
@@ -149,6 +149,19 @@
         yb[3 * f : 3 * f + 3, :] = u[f, ny - 3 : ny, :]
     yt[15:16, :] = u[0, 0:1, :]
     yb[15:16, :] = u[0, 0:1, :]
+    up, down = shifts(nx, 1)
+
+    def sweep_tile(at):
+        profiles = primitives([u[f, at, :] for f in range(5)])
+        for f, difference in enumerate(flux_differences(profiles, up, down, 1)):
+            df[f, at, :] = difference
+
+    deep = 2 * SUBLANES if ny % (2 * SUBLANES) == 0 else SUBLANES
+
+    @pl.loop(0, ny // deep)
+    def _(tile):
+        sweep_tile(pl.ds(pl.multiple_of(tile * deep, deep), deep))
+
     pl.semaphore_wait(barrier, count - 1 + len(near))
     pair = pltpu.make_async_remote_copy(
         src_ref=mine, dst_ref=theirs, send_sem=pair_send, recv_sem=pair_recv,
@@ -188,19 +201,6 @@
 
     for_chips(tell)
 
-    up, down = shifts(nx, 1)
-
-    def sweep_tile(at):
-        profiles = primitives([u[f, at, :] for f in range(5)])
-        for f, difference in enumerate(flux_differences(profiles, up, down, 1)):
-            df[f, at, :] = difference
-
-    deep = 2 * SUBLANES if ny % (2 * SUBLANES) == 0 else SUBLANES
-
-    @pl.loop(0, ny // deep)
-    def _(tile):
-        sweep_tile(pl.ds(pl.multiple_of(tile * deep, deep), deep))
-
     for copy in halos:
         copy.wait_recv()
     for f in range(5):

time: 11.6 us -> 12 us (1.034)
  Pallas kernels: 10.7 us -> 11.2 us
    pallas_call x1, Pallas kernels: 10.7 us -> 11.2 us  [local(): pl.pallas_call(functools.partial(kernel, rows, cols), out_shape=jax.Shape...]
where the time goes in v10:
time: 12 us; the launch traced here: 11.9 us
  Pallas kernels  11.2 us (93%)
  local copies, waits for them, and re-layouts  0.67 us (6%)
    pallas_call x1, Pallas kernels, local(): pl.pallas_call(functools.partial(kernel, rows, cols), out_shape=jax.Shape...  11.2 us
    unnamed x1, local copies, waits for them, and re-layouts  0.67 us

profile of v10, /device:TPU:0, one launch (start us, length us, event | category | flops | bytes accessed | tf_op | source)
XLA Modules:
  0.0 11.9 jit_solution(11149567699198640030)
XLA Ops:
  0.0 11.2 %sweeps.1 = f32[5,1,16,512]{3,2,1,0:T(8,128)S(1)} custom-call(f32[5,1,16,512]{3,2,1,0:T(8,128)} %x.1), custom_call_target="tpu_custom_call" | custom-call | tf_op jit(solution)/shard_map/sweeps/pallas_call | solution.py:262
  11.2 0.7 %copy.3 = f32[5,1,16,512]{3,2,1,0:T(8,128)} copy(f32[5,1,16,512]{3,2,1,0:T(8,128)S(1)} %sweeps.1) | data formatting | bytes 327680

commit v11 on v9

--- a/solution.py
+++ b/solution.py
@@ -78,8 +78,8 @@
 
 
 def kernel(
-    rows, cols, x, out, u, df, xr, xl, yt, yb, rxl, rxr, rya, ryb, rc, mine, theirs, both, others,
-    in_sem, halo_send, halo_recv, pair_send, pair_recv, peak_send, peak_recv,
+    rows, cols, x, out, u, df, xr, xl, yt, yb, rxl, rxr, rya, ryb, rc, mine, others,
+    in_sem, halo_send, halo_recv, peak_send, peak_recv,
 ):
     ny, nx = x.shape[2], x.shape[3]
     me_r, me_c = lax.axis_index("row"), lax.axis_index("col")
@@ -94,31 +94,24 @@
     load.start()
 
     barrier = pltpu.get_barrier_semaphore()
-    partner = (me_r, me_c + 1 - 2 * lax.rem(me_c, 2))
-    half = cols // 2
-    count = rows * half
-
-    def for_chips(act):
+    count = rows * cols
+
+    def for_peers(act):
         if count <= UNROLLED:
             at_row = [row_at(a) for a in range(rows)]
-            at_col = [col_at(2 * b) for b in range(half)]
+            at_col = [col_at(b) for b in range(cols)]
             for d in range(1, count):
-                act(d, (at_row[d // half], at_col[d % half]))
+                act(d, (at_row[d // cols], at_col[d % cols]))
         else:
 
             @pl.loop(1, count)
             def _(d):
-                step = 2 * (d % half)
-                act(d, (lax.rem(me_r + d // half, rows), lax.rem(me_c + step, cols)))
+                act(d, (lax.rem(me_r + d // cols, rows), lax.rem(me_c + d % cols, cols)))
 
     def greet(d, peer):
         pl.semaphore_signal(barrier, inc=1, device_id=peer, device_id_type=MESH)
 
-    near = [(me_r, col_at(b)) for b in (1, -1)]
-    near += [(row_at(a), col_at(b)) for a in (1, -1) for b in (1, -1)]
-    for peer in near:
-        greet(0, peer)
-    for_chips(greet)
+    for_peers(greet)
     load.wait()
 
     peak = None
@@ -129,14 +122,8 @@
         for c in range(0, nx, LANES):
             part = speed[:, c : c + LANES]
             peak = part if peak is None else jnp.maximum(peak, part)
-    mine[...] = jnp.max(peak, axis=0, keepdims=True)
-
-    pl.semaphore_wait(barrier, count - 1 + len(near))
-    pair = pltpu.make_async_remote_copy(
-        src_ref=mine, dst_ref=theirs, send_sem=pair_send, recv_sem=pair_recv,
-        device_id=partner, device_id_type=MESH,
-    )
-    pair.start()
+    peak = jnp.max(jnp.max(peak, axis=0, keepdims=True), axis=1, keepdims=True)
+    mine[...] = jnp.broadcast_to(peak, mine.shape)
 
     lane = lax.broadcasted_iota(jnp.int32, (ny, LANES), 1)
     pack_r = pack_l = None
@@ -156,6 +143,15 @@
         yb[3 * f : 3 * f + 3, :] = u[f, ny - 3 : ny, :]
     yt[15:16, :] = u[0, 0:1, :]
     yb[15:16, :] = u[0, 0:1, :]
+    pl.semaphore_wait(barrier, count - 1)
+
+    def tell(d, peer):
+        pltpu.make_async_remote_copy(
+            src_ref=mine, dst_ref=others.at[d - 1], send_sem=peak_send, recv_sem=peak_recv,
+            device_id=peer, device_id_type=MESH,
+        ).start()
+
+    for_peers(tell)
     top, bottom = pl.ds(0, SUBLANES), pl.ds(ny - SUBLANES, SUBLANES)
     halos = []
     for i, (src, dst, device) in enumerate(
@@ -178,17 +174,6 @@
         )
         halos[i].start()
 
-    pair.wait_recv()
-    both[...] = jnp.maximum(mine[...], theirs[...])
-
-    def tell(d, peer):
-        pltpu.make_async_remote_copy(
-            src_ref=both, dst_ref=others.at[d - 1], send_sem=peak_send, recv_sem=peak_recv,
-            device_id=peer, device_id_type=MESH,
-        ).start()
-
-    for_chips(tell)
-
     up, down = shifts(nx, 1)
 
     def sweep_tile(at):
@@ -233,13 +218,13 @@
         )
 
     pltpu.make_async_copy(others, others, peak_recv).wait()
-    peak = jnp.maximum(both[...], jnp.max(others[...], axis=0))
-    peak = jnp.max(peak, axis=1, keepdims=True)
+    peak = jnp.maximum(mine[...], jnp.max(others[...], axis=0))
     half_step = (0.5 * COURANT) / peak
 
     up, down = shifts(total, 0)
 
     wide = 2 * LANES if nx % (2 * LANES) == 0 else LANES
+    half_step = jnp.concatenate([half_step] * (wide // LANES), axis=1)
 
     @pl.loop(0, nx // wide)
     def _(chunk):
@@ -252,7 +237,6 @@
 
     for copy in halos:
         copy.wait_send()
-    pair.wait_send()
     pltpu.make_async_copy(others, others, peak_send).wait()
 
 
@@ -278,14 +262,10 @@
             vmem(16, nx),
             vmem(4, SUBLANES, LANES),
             vmem(1, LANES),
-            vmem(1, LANES),
-            vmem(1, LANES),
-            vmem(rows * cols // 2 - 1, 1, LANES),
+            vmem(rows * cols - 1, 1, LANES),
             dma,
             dma((8,)),
             dma((8,)),
-            dma,
-            dma,
             dma,
             dma,
         ],

time: 11.6 us -> 11.5 us (level)
  no operation moved by 1% of the time
where the time goes in v11:
time: 11.5 us; the launch traced here: 11.4 us
  Pallas kernels  10.7 us (93%)
  local copies, waits for them, and re-layouts  0.67 us (6%)
    pallas_call x1, Pallas kernels, local(): pl.pallas_call(functools.partial(kernel, rows, cols), out_shape=jax.Shape...  10.7 us
    unnamed x1, local copies, waits for them, and re-layouts  0.67 us

profile of v11, /device:TPU:0, one launch (start us, length us, event | category | flops | bytes accessed | tf_op | source)
XLA Modules:
  0.0 11.4 jit_solution(1329909598486696445)
XLA Ops:
  0.0 10.7 %sweeps.1 = f32[5,1,16,512]{3,2,1,0:T(8,128)S(1)} custom-call(f32[5,1,16,512]{3,2,1,0:T(8,128)} %x.1), custom_call_target="tpu_custom_call" | custom-call | tf_op jit(solution)/shard_map/sweeps/pallas_call | solution.py:247
  10.7 0.7 %copy.3 = f32[5,1,16,512]{3,2,1,0:T(8,128)} copy(f32[5,1,16,512]{3,2,1,0:T(8,128)S(1)} %sweeps.1) | data formatting | bytes 327680

commit v12 on v11

--- a/solution.py
+++ b/solution.py
@@ -151,7 +151,6 @@
             device_id=peer, device_id_type=MESH,
         ).start()
 
-    for_peers(tell)
     top, bottom = pl.ds(0, SUBLANES), pl.ds(ny - SUBLANES, SUBLANES)
     halos = []
     for i, (src, dst, device) in enumerate(
@@ -173,6 +172,8 @@
             )
         )
         halos[i].start()
+        if i == 1:
+            for_peers(tell)
 
     up, down = shifts(nx, 1)
 

time: 11.5 us -> 11.5 us (level)
  no operation moved by 1% of the time
where the time goes in v12:
time: 11.5 us; the launch traced here: 11.3 us
  Pallas kernels  10.7 us (93%)
  local copies, waits for them, and re-layouts  0.67 us (6%)
    pallas_call x1, Pallas kernels, local(): pl.pallas_call(functools.partial(kernel, rows, cols), out_shape=jax.Shape...  10.7 us
    unnamed x1, local copies, waits for them, and re-layouts  0.67 us

profile of v12, /device:TPU:0, one launch (start us, length us, event | category | flops | bytes accessed | tf_op | source)
XLA Modules:
  0.0 11.3 jit_solution(5056068817501092893)
XLA Ops:
  0.0 10.7 %sweeps.1 = f32[5,1,16,512]{3,2,1,0:T(8,128)S(1)} custom-call(f32[5,1,16,512]{3,2,1,0:T(8,128)} %x.1), custom_call_target="tpu_custom_call" | custom-call | tf_op jit(solution)/shard_map/sweeps/pallas_call | solution.py:248
  10.7 0.7 %copy.3 = f32[5,1,16,512]{3,2,1,0:T(8,128)} copy(f32[5,1,16,512]{3,2,1,0:T(8,128)S(1)} %sweeps.1) | data formatting | bytes 327680

commit v13 on v11

--- a/solution.py
+++ b/solution.py
@@ -187,14 +187,16 @@
     def _(tile):
         sweep_tile(pl.ds(pl.multiple_of(tile * deep, deep), deep))
 
-    for copy in halos:
-        copy.wait_recv()
+    halos[0].wait_recv()
+    halos[1].wait_recv()
     for f in range(5):
         u[f, ny : ny + 3, :] = ryb[3 * f : 3 * f + 3, :]
         u[f, ny + 3 : ny + 5, :] = u[f, 3:5, :]
         u[f, ny + 5 : ny + 8, :] = rya[3 * f : 3 * f + 3, :]
     sweep_tile(pl.ds(ny, SUBLANES))
 
+    for copy in halos[2:]:
+        copy.wait_recv()
     total = ny + SUBLANES
     lane = lax.broadcasted_iota(jnp.int32, (total, LANES), 1)
     below = lax.broadcasted_iota(jnp.int32, (SUBLANES, LANES), 0) < 4
@@ -226,9 +228,8 @@
     wide = 2 * LANES if nx % (2 * LANES) == 0 else LANES
     half_step = jnp.concatenate([half_step] * (wide // LANES), axis=1)
 
-    @pl.loop(0, nx // wide)
-    def _(chunk):
-        at = pl.ds(pl.multiple_of(chunk * wide, wide), wide)
+    for begin in range(0, nx, wide):
+        at = pl.ds(begin, wide)
         cells = [u[f, :, at] - half_step * df[f, :, at] for f in range(5)]
         profiles = primitives(cells)
         for f, difference in enumerate(flux_differences(profiles, up, down, 2)):

time: 11.5 us -> 11.6 us (level)
  the two profiles are of different devices: /device:TPU:0 before, /device:TPU:1 now
where the time goes in v13:
time: 11.6 us; the launch traced here: 11.4 us
  Pallas kernels  10.8 us (93%)
  local copies, waits for them, and re-layouts  0.67 us (6%)
    pallas_call x1, Pallas kernels, local(): pl.pallas_call(functools.partial(kernel, rows, cols), out_shape=jax.Shape...  10.8 us
    unnamed x1, local copies, waits for them, and re-layouts  0.67 us

profile of v13, /device:TPU:1, one launch (start us, length us, event | category | flops | bytes accessed | tf_op | source)
XLA Modules:
  0.0 11.4 jit_solution(9662543318958928926)
XLA Ops:
  0.0 10.8 %sweeps.1 = f32[5,1,16,512]{3,2,1,0:T(8,128)S(1)} custom-call(f32[5,1,16,512]{3,2,1,0:T(8,128)} %x.1), custom_call_target="tpu_custom_call" | custom-call | tf_op jit(solution)/shard_map/sweeps/pallas_call | solution.py:248
  10.8 0.7 %copy.3 = f32[5,1,16,512]{3,2,1,0:T(8,128)} copy(f32[5,1,16,512]{3,2,1,0:T(8,128)S(1)} %sweeps.1) | data formatting | bytes 327680

commit v14 on v13

--- a/solution.py
+++ b/solution.py
@@ -151,7 +151,6 @@
             device_id=peer, device_id_type=MESH,
         ).start()
 
-    for_peers(tell)
     top, bottom = pl.ds(0, SUBLANES), pl.ds(ny - SUBLANES, SUBLANES)
     halos = []
     for i, (src, dst, device) in enumerate(
@@ -172,7 +171,23 @@
                 device_id=device, device_id_type=MESH,
             )
         )
-        halos[i].start()
+
+    first, last = me_c == 0, me_c == cols - 1
+    downward, upward = (halos[0], halos[4], halos[5]), (halos[1], halos[6], halos[7])
+
+    def start_when(condition, copies):
+        @pl.when(condition)
+        def _():
+            for copy in copies:
+                copy.start()
+
+    start_when(last, downward)
+    start_when(first, upward)
+    for_peers(tell)
+    start_when(jnp.logical_not(last), downward)
+    start_when(jnp.logical_not(first), upward)
+    halos[2].start()
+    halos[3].start()
 
     up, down = shifts(nx, 1)
 

time: 11.6 us -> 11.6 us (level)
  the two profiles are of different devices: /device:TPU:1 before, /device:TPU:0 now
where the time goes in v14:
time: 11.6 us; the launch traced here: 11.4 us
  Pallas kernels  10.7 us (92%)
  local copies, waits for them, and re-layouts  0.67 us (6%)
    pallas_call x1, Pallas kernels, local(): pl.pallas_call(functools.partial(kernel, rows, cols), out_shape=jax.Shape...  10.7 us
    unnamed x1, local copies, waits for them, and re-layouts  0.67 us

profile of v14, /device:TPU:0, one launch (start us, length us, event | category | flops | bytes accessed | tf_op | source)
XLA Modules:
  0.0 11.4 jit_solution(566855981457197037)
XLA Ops:
  0.0 10.7 %sweeps.1 = f32[5,1,16,512]{3,2,1,0:T(8,128)S(1)} custom-call(f32[5,1,16,512]{3,2,1,0:T(8,128)} %x.1), custom_call_target="tpu_custom_call" | custom-call | tf_op jit(solution)/shard_map/sweeps/pallas_call | solution.py:263
  10.7 0.7 %copy.3 = f32[5,1,16,512]{3,2,1,0:T(8,128)} copy(f32[5,1,16,512]{3,2,1,0:T(8,128)S(1)} %sweeps.1) | data formatting | bytes 327680

commit v15 on v8

--- a/solution.py
+++ b/solution.py
@@ -129,7 +129,8 @@
         for c in range(0, nx, LANES):
             part = speed[:, c : c + LANES]
             peak = part if peak is None else jnp.maximum(peak, part)
-    mine[...] = jnp.max(peak, axis=0, keepdims=True)
+    peak = jnp.max(jnp.max(peak, axis=0, keepdims=True), axis=1, keepdims=True)
+    mine[...] = jnp.broadcast_to(peak, mine.shape)
 
     lane = lax.broadcasted_iota(jnp.int32, (ny, LANES), 1)
     pack_r = pack_l = None
@@ -155,6 +156,17 @@
         device_id=partner, device_id_type=MESH,
     )
     pair.start()
+    pair.wait_recv()
+    both[...] = jnp.maximum(mine[...], theirs[...])
+
+    def tell(d, peer):
+        pltpu.make_async_remote_copy(
+            src_ref=both, dst_ref=others.at[d - 1], send_sem=peak_send, recv_sem=peak_recv,
+            device_id=peer, device_id_type=MESH,
+        ).start()
+
+    for_chips(tell)
+
     top, bottom = pl.ds(0, SUBLANES), pl.ds(ny - SUBLANES, SUBLANES)
     halos = []
     for i, (src, dst, device) in enumerate(
@@ -177,17 +189,6 @@
         )
         halos[i].start()
 
-    pair.wait_recv()
-    both[...] = jnp.maximum(mine[...], theirs[...])
-
-    def tell(d, peer):
-        pltpu.make_async_remote_copy(
-            src_ref=both, dst_ref=others.at[d - 1], send_sem=peak_send, recv_sem=peak_recv,
-            device_id=peer, device_id_type=MESH,
-        ).start()
-
-    for_chips(tell)
-
     up, down = shifts(nx, 1)
 
     def sweep_tile(at):
@@ -201,14 +202,16 @@
     def _(tile):
         sweep_tile(pl.ds(pl.multiple_of(tile * deep, deep), deep))
 
-    for copy in halos:
-        copy.wait_recv()
+    halos[0].wait_recv()
+    halos[1].wait_recv()
     for f in range(5):
         u[f, ny : ny + 3, :] = ryb[3 * f : 3 * f + 3, :]
         u[f, ny + 3 : ny + 5, :] = u[f, 3:5, :]
         u[f, ny + 5 : ny + 8, :] = rya[3 * f : 3 * f + 3, :]
     sweep_tile(pl.ds(ny, SUBLANES))
 
+    for copy in halos[2:]:
+        copy.wait_recv()
     total = ny + SUBLANES
     lane = lax.broadcasted_iota(jnp.int32, (total, LANES), 1)
     below = lax.broadcasted_iota(jnp.int32, (SUBLANES, LANES), 0) < 4
@@ -233,12 +236,12 @@
 
     pltpu.make_async_copy(others, others, peak_recv).wait()
     peak = jnp.maximum(both[...], jnp.max(others[...], axis=0))
-    peak = jnp.max(peak, axis=1, keepdims=True)
     half_step = (0.5 * COURANT) / peak
 
     up, down = shifts(total, 0)
 
     wide = 2 * LANES if nx % (2 * LANES) == 0 else LANES
+    half_step = jnp.concatenate([half_step] * (wide // LANES), axis=1)
 
     @pl.loop(0, nx // wide)
     def _(chunk):

time: 11.6 us -> 12.9 us (1.11)
  Pallas kernels: 10.7 us -> 12.1 us
    pallas_call x1, Pallas kernels: 10.7 us -> 12.1 us  [local(): pl.pallas_call(functools.partial(kernel, rows, cols), out_shape=jax.Shape...]
where the time goes in v15:
time: 12.9 us; the launch traced here: 12.7 us
  Pallas kernels  12.1 us (94%)
  local copies, waits for them, and re-layouts  0.67 us (5%)
    pallas_call x1, Pallas kernels, local(): pl.pallas_call(functools.partial(kernel, rows, cols), out_shape=jax.Shape...  12.1 us
    unnamed x1, local copies, waits for them, and re-layouts  0.67 us

profile of v15, /device:TPU:0, one launch (start us, length us, event | category | flops | bytes accessed | tf_op | source)
XLA Modules:
  0.0 12.7 jit_solution(16302719806680317402)
XLA Ops:
  0.0 12.1 %sweeps.1 = f32[5,1,16,512]{3,2,1,0:T(8,128)S(1)} custom-call(f32[5,1,16,512]{3,2,1,0:T(8,128)} %x.1), custom_call_target="tpu_custom_call" | custom-call | tf_op jit(solution)/shard_map/sweeps/pallas_call | solution.py:265
  12.1 0.7 %copy.3 = f32[5,1,16,512]{3,2,1,0:T(8,128)} copy(f32[5,1,16,512]{3,2,1,0:T(8,128)S(1)} %sweeps.1) | data formatting | bytes 327680

commit v16 on v8

--- a/solution.py
+++ b/solution.py
@@ -129,7 +129,8 @@
         for c in range(0, nx, LANES):
             part = speed[:, c : c + LANES]
             peak = part if peak is None else jnp.maximum(peak, part)
-    mine[...] = jnp.max(peak, axis=0, keepdims=True)
+    peak = jnp.max(jnp.max(peak, axis=0, keepdims=True), axis=1, keepdims=True)
+    mine[...] = jnp.broadcast_to(peak, mine.shape)
 
     lane = lax.broadcasted_iota(jnp.int32, (ny, LANES), 1)
     pack_r = pack_l = None
@@ -201,14 +202,16 @@
     def _(tile):
         sweep_tile(pl.ds(pl.multiple_of(tile * deep, deep), deep))
 
-    for copy in halos:
-        copy.wait_recv()
+    halos[0].wait_recv()
+    halos[1].wait_recv()
     for f in range(5):
         u[f, ny : ny + 3, :] = ryb[3 * f : 3 * f + 3, :]
         u[f, ny + 3 : ny + 5, :] = u[f, 3:5, :]
         u[f, ny + 5 : ny + 8, :] = rya[3 * f : 3 * f + 3, :]
     sweep_tile(pl.ds(ny, SUBLANES))
 
+    for copy in halos[2:]:
+        copy.wait_recv()
     total = ny + SUBLANES
     lane = lax.broadcasted_iota(jnp.int32, (total, LANES), 1)
     below = lax.broadcasted_iota(jnp.int32, (SUBLANES, LANES), 0) < 4
@@ -233,12 +236,12 @@
 
     pltpu.make_async_copy(others, others, peak_recv).wait()
     peak = jnp.maximum(both[...], jnp.max(others[...], axis=0))
-    peak = jnp.max(peak, axis=1, keepdims=True)
     half_step = (0.5 * COURANT) / peak
 
     up, down = shifts(total, 0)
 
     wide = 2 * LANES if nx % (2 * LANES) == 0 else LANES
+    half_step = jnp.concatenate([half_step] * (wide // LANES), axis=1)
 
     @pl.loop(0, nx // wide)
     def _(chunk):

time: 11.6 us -> 11.5 us (level)
  no operation moved by 1% of the time
where the time goes in v16:
time: 11.5 us; the launch traced here: 11.4 us
  Pallas kernels  10.7 us (93%)
  local copies, waits for them, and re-layouts  0.67 us (6%)
    pallas_call x1, Pallas kernels, local(): pl.pallas_call(functools.partial(kernel, rows, cols), out_shape=jax.Shape...  10.7 us
    unnamed x1, local copies, waits for them, and re-layouts  0.67 us

profile of v16, /device:TPU:0, one launch (start us, length us, event | category | flops | bytes accessed | tf_op | source)
XLA Modules:
  0.0 11.4 jit_solution(12516462496983831125)
XLA Ops:
  0.0 10.7 %sweeps.1 = f32[5,1,16,512]{3,2,1,0:T(8,128)S(1)} custom-call(f32[5,1,16,512]{3,2,1,0:T(8,128)} %x.1), custom_call_target="tpu_custom_call" | custom-call | tf_op jit(solution)/shard_map/sweeps/pallas_call | solution.py:265
  10.7 0.7 %copy.3 = f32[5,1,16,512]{3,2,1,0:T(8,128)} copy(f32[5,1,16,512]{3,2,1,0:T(8,128)S(1)} %sweeps.1) | data formatting | bytes 327680
